TPU v7x, 256 devices: a whole 4x4x8 slice. The times are simulated.
256 devices in a mesh: ctx: 32 (over z, y), tp: 8 (over x, core).
Axes of the slice: x: 4, y: 4, z: 8, core: 2. Of those that a mesh axis runs over, the one named last changes fastest.
Arguments:
- lin_query: bfloat16 [8192, 4096], P('ctx', 'tp'), may hold values from -6 to 6
- lin_key: bfloat16 [8192, 4096], P('ctx', 'tp'), may hold values from -0.35 to 0.35
- lin_value: bfloat16 [8192, 4096], P('ctx', 'tp'), may hold values from -7 to 7
- log_decay: float32 [32, 8192], P('tp', 'ctx'), may hold values from -1 to 0
- norm_gain: float32 [4096], P('tp'), may hold values from 0.5 to 1.5
- lin_gate: bfloat16 [8192, 4096], P('ctx', 'tp'), may hold values from -6 to 6
- lin_grad: bfloat16 [8192, 4096], P('ctx', 'tp'), may hold values from -6 to 6
- soft_query: bfloat16 [8192, 4096], P('ctx', 'tp'), may hold values from -6 to 6
- soft_key: bfloat16 [8192, 1024], P('ctx', 'tp'), may hold values from -6 to 6
- soft_value: bfloat16 [8192, 1024], P('ctx', 'tp'), may hold values from -6 to 6
- soft_grad: bfloat16 [8192, 4096], P('ctx', 'tp'), may hold values from -6 to 6
Outputs:
- lin_out: bfloat16 [8192, 4096], P('ctx', 'tp')
- lin_query_grad: bfloat16 [8192, 4096], P('ctx', 'tp')
- lin_key_grad: bfloat16 [8192, 4096], P('ctx', 'tp')
- lin_value_grad: bfloat16 [8192, 4096], P('ctx', 'tp')
- lin_gate_grad: bfloat16 [8192, 4096], P('ctx', 'tp')
- soft_out: bfloat16 [8192, 4096], P('ctx', 'tp')
- soft_query_grad: bfloat16 [8192, 4096], P('ctx', 'tp')
- soft_key_grad: bfloat16 [8192, 1024], P('ctx', 'tp')
- soft_value_grad: bfloat16 [8192, 1024], P('ctx', 'tp')
All inputs are finite; a program needn't handle non-finite values.
Results may differ from a plain program's by a relative error of at most 0.035.
Values may be sent and summed in bfloat16 or wider, within the bound.
A program may use at most 128 MiB of HBM per device.

v0:
```python
import jax
import jax.numpy as jnp
from jax import lax
from jax.sharding import PartitionSpec as P

DH = 128
LINEAR_HEADS = 32


negative_fill = -1e30
top_precision = lax.Precision.HIGHEST


def carried_in(shard, axis, join, neutral, backward):
    count = lax.axis_size(axis)
    place = lax.axis_index(axis)
    ahead = count - 1 - place if backward else place
    gathered = jax.tree.map(
        lambda a, kind: lax.all_gather(a.astype(kind), axis), shard, (jnp.bfloat16, jnp.bfloat16)
    )
    state = jax.tree.map(lambda a, e: jnp.zeros_like(a) + jnp.asarray(e, a.dtype), shard, neutral)

    def one(lap, state):
        source = count - 1 - lap if backward else lap
        return join(
            state,
            jax.tree.map(
                lambda a, own: lax.dynamic_index_in_dim(a, source, 0, False).astype(own.dtype),
                gathered,
                shard,
            ),
        )

    return lax.fori_loop(0, ahead, one, state)


def combine_state(earlier, later):
    return (earlier[0] + later[0], jnp.exp(later[0])[:, None, None] * earlier[1] + later[1])


def lightning(lin_query, lin_key, lin_value, log_decay, norm_gain, lin_gate, lin_grad):
    row_count = lin_query.shape[0]
    head_count = lin_query.shape[1] // DH
    query3 = lin_query.reshape(row_count, head_count, DH)
    key3 = lin_key.reshape(row_count, head_count, DH)
    value3 = lin_value.reshape(row_count, head_count, DH)
    blocklog = jnp.cumsum(log_decay, axis=1)
    totals = blocklog[:, -1]
    order_ids = jnp.arange(row_count)
    causal = (order_ids[:, None] >= order_ids[None, :])[None]
    spread = blocklog[:, :, None] - blocklog[:, None, :]
    decay_mask = jnp.where(causal, jnp.exp(jnp.where(causal, spread, 0.0)), 0.0)
    tail_decay = jnp.exp(totals[:, None] - blocklog).T[:, :, None]
    lead_decay = jnp.exp(blocklog).T[:, :, None]
    raw_scores = jnp.einsum("thd,shd->hts", query3, key3, preferred_element_type=jnp.float32)
    weights = (raw_scores * decay_mask).astype(jnp.bfloat16)
    key_tail = key3.astype(jnp.float32) * tail_decay
    value_f = value3.astype(jnp.float32)
    query_lead = query3.astype(jnp.float32) * lead_decay
    local_state = jnp.einsum("shd,she->hde", key_tail, value_f, precision=top_precision)
    identity = (jnp.zeros_like(totals), jnp.zeros_like(local_state))
    carried = carried_in((totals, local_state), "ctx", combine_state, identity, False)[1]
    attended = jnp.einsum("hts,she->the", weights, value3, preferred_element_type=jnp.float32)
    attended = attended + jnp.einsum("thd,hde->the", query_lead, carried, precision=top_precision)
    flat_out = attended.reshape(row_count, head_count * DH)
    squares = lax.psum(jnp.sum(flat_out * flat_out, axis=1), "tp")
    scaling = lax.rsqrt(squares / (LINEAR_HEADS * DH) + 1e-05)[:, None]
    normed = flat_out * scaling
    gate_sig = jax.nn.sigmoid(lin_gate.astype(jnp.float32))
    gain_row = norm_gain[None, :]
    lin_out = (normed * gain_row * gate_sig).astype(jnp.bfloat16)
    grad_f = lin_grad.astype(jnp.float32)
    scaled = grad_f * gain_row * gate_sig
    gate_grad = (grad_f * normed * gain_row * gate_sig * (1.0 - gate_sig)).astype(jnp.bfloat16)
    cross_term = lax.psum(jnp.sum(scaled * normed, axis=1), "tp")
    att_grad = (scaling * (scaled - normed * (cross_term / (LINEAR_HEADS * DH))[:, None])).astype(
        jnp.bfloat16
    )
    grad3 = att_grad.reshape(row_count, head_count, DH)
    grad_weights = (
        jnp.einsum("the,she->hts", grad3, value3, preferred_element_type=jnp.float32) * decay_mask
    ).astype(jnp.bfloat16)
    grad_lead = grad3.astype(jnp.float32) * lead_decay
    local_grad = jnp.einsum(
        "thd,the->hde", query_lead, grad3.astype(jnp.float32), precision=top_precision
    )
    grad_identity = (jnp.zeros_like(totals), jnp.zeros_like(local_grad))
    returned = carried_in((totals, local_grad), "ctx", combine_state, grad_identity, True)[1]
    query_grad = jnp.einsum("hts,shd->thd", grad_weights, key3, preferred_element_type=jnp.float32)
    query_grad = query_grad + jnp.einsum(
        "the,hde->thd", grad_lead, carried, precision=top_precision
    )
    key_grad = jnp.einsum("hts,thd->shd", grad_weights, query3, preferred_element_type=jnp.float32)
    key_grad = key_grad + jnp.einsum(
        "she,hde->shd", value_f * tail_decay, returned, precision=top_precision
    )
    value_grad = jnp.einsum("hts,the->she", weights, grad3, preferred_element_type=jnp.float32)
    value_grad = value_grad + jnp.einsum(
        "shd,hde->she", key_tail, returned, precision=top_precision
    )
    width = head_count * DH
    return (
        lin_out,
        query_grad.reshape(row_count, width).astype(jnp.bfloat16),
        key_grad.reshape(row_count, width).astype(jnp.bfloat16),
        value_grad.reshape(row_count, width).astype(jnp.bfloat16),
        gate_grad,
    )


def key_tiles(keys_all, values_all, start_row, piece_rows):
    kv_heads = keys_all.shape[1] // DH
    key_tile = lax.dynamic_slice_in_dim(keys_all, start_row, piece_rows, 0).reshape(
        piece_rows, kv_heads, DH
    )
    value_tile = lax.dynamic_slice_in_dim(values_all, start_row, piece_rows, 0).reshape(
        piece_rows, kv_heads, DH
    )
    return (key_tile, value_tile)


def half_forward(query4, positions, last_row, keys_all, values_all, block_rows):
    score_scale = DH ** (-0.5)
    half_rows, kv_heads, group_size = (query4.shape[0], query4.shape[1], query4.shape[2])
    block_count = keys_all.shape[0] // block_rows

    def keep_same(current):
        return current

    def half_block_step(running, block_index):
        start_row = block_index * block_rows

        def half_compute(current):
            row_peak, row_total, accumulated = current
            key_tile, value_tile = key_tiles(keys_all, values_all, start_row, block_rows)
            scores = (
                jnp.einsum("rkgd,ckd->kgrc", query4, key_tile, preferred_element_type=jnp.float32)
                * score_scale
            )
            allowed = positions[:, None] >= (start_row + jnp.arange(block_rows))[None, :]
            fresh_peak = jnp.maximum(
                row_peak, jnp.max(jnp.where(allowed, scores, negative_fill), axis=-1)
            )
            probs = jnp.where(allowed, jnp.exp(scores - fresh_peak[..., None]), 0.0)
            correction = jnp.exp(row_peak - fresh_peak)
            row_total = row_total * correction + jnp.sum(probs, axis=-1)
            product = jnp.einsum(
                "kgrc,ckd->kgrd",
                probs.astype(jnp.bfloat16),
                value_tile,
                preferred_element_type=jnp.float32,
            )
            accumulated = accumulated * correction[..., None] + product
            return (fresh_peak, row_total, accumulated)

        return (lax.cond(start_row <= last_row, half_compute, keep_same, running), None)

    initial = (
        jnp.full((kv_heads, group_size, half_rows), negative_fill, jnp.float32),
        jnp.zeros((kv_heads, group_size, half_rows), jnp.float32),
        jnp.zeros((kv_heads, group_size, half_rows, DH), jnp.float32),
    )
    final_state, _ = lax.scan(half_block_step, initial, jnp.arange(block_count))
    return final_state


def block_grads(half_data, start_row, piece_rows, keys_all, values_all):
    score_scale = DH ** (-0.5)
    query4, grad_block, positions, last_row, logsum, delta_rows = half_data
    key_tile, value_tile = key_tiles(keys_all, values_all, start_row, piece_rows)
    scores = (
        jnp.einsum("rkgd,ckd->kgrc", query4, key_tile, preferred_element_type=jnp.float32)
        * score_scale
    )
    allowed = positions[:, None] >= (start_row + jnp.arange(piece_rows))[None, :]
    probs = jnp.where(allowed, jnp.exp(scores - logsum[..., None]), 0.0)
    prob_grad = jnp.einsum(
        "rkgd,ckd->kgrc", grad_block, value_tile, preferred_element_type=jnp.float32
    )
    score_grad = (probs * (prob_grad - delta_rows[..., None])).astype(jnp.bfloat16)
    results = []
    results.append(
        jnp.einsum("kgrc,ckd->kgrd", score_grad, key_tile, preferred_element_type=jnp.float32)
        * score_scale
    )
    results.append(
        jnp.einsum("kgrc,rkgd->ckd", score_grad, query4, preferred_element_type=jnp.float32)
        * score_scale
    )
    results.append(
        jnp.einsum(
            "kgrc,rkgd->ckd",
            probs.astype(jnp.bfloat16),
            grad_block,
            preferred_element_type=jnp.float32,
        )
    )
    return tuple(results)


def guarded_grads(half_data, start_row, piece_rows, keys_all, values_all):
    query4 = half_data[0]
    half_rows, kv_heads, group_size = (query4.shape[0], query4.shape[1], query4.shape[2])
    zero_query = jnp.zeros((kv_heads, group_size, half_rows, DH), jnp.float32)
    zero_keys = jnp.zeros((piece_rows, kv_heads, DH), jnp.float32)
    empty_terms = (zero_query, zero_keys, zero_keys)

    def guarded_compute():
        return block_grads(half_data, start_row, piece_rows, keys_all, values_all)

    def skip_block():
        return empty_terms

    return lax.cond(start_row <= half_data[3], guarded_compute, skip_block)


def soft_attention(query_rows, keys_all, values_all, grad_rows, starts):
    row_count = query_rows.shape[0]
    half_rows = row_count // 2
    query_width = query_rows.shape[1]
    kv_heads = keys_all.shape[1] // DH
    group_size = query_width // DH // kv_heads
    key_count = keys_all.shape[0]
    block_rows = max(min(512, key_count), key_count // 16)
    block_count = key_count // block_rows
    halves = []
    out_halves = []
    for half_index in range(2):
        lower_row = half_index * half_rows
        upper_row = lower_row + half_rows
        query4 = query_rows[lower_row:upper_row].reshape(half_rows, kv_heads, group_size, DH)
        grad_block = grad_rows[lower_row:upper_row].reshape(half_rows, kv_heads, group_size, DH)
        positions = starts[half_index] + jnp.arange(half_rows)
        last_row = starts[half_index] + half_rows - 1
        row_peak, row_total, accumulated = half_forward(
            query4, positions, last_row, keys_all, values_all, block_rows
        )
        out_half = (
            (accumulated / row_total[..., None])
            .transpose(2, 0, 1, 3)
            .reshape(half_rows, query_width)
            .astype(jnp.bfloat16)
        )
        logsum = row_peak + jnp.log(row_total)
        out_back = (
            lax.optimization_barrier(out_half)
            .astype(jnp.float32)
            .reshape(half_rows, kv_heads, group_size, DH)
        )
        delta_rows = jnp.sum(grad_block.astype(jnp.float32) * out_back, axis=-1).transpose(1, 2, 0)
        halves.append((query4, grad_block, positions, last_row, logsum, delta_rows))
        out_halves.append(out_half)
    key_width = kv_heads * DH
    zero_query = jnp.zeros((kv_heads, group_size, half_rows, DH), jnp.float32)

    def soft_block_step(running, block_index):
        start_row = block_index * block_rows
        first_part = guarded_grads(halves[0], start_row, block_rows, keys_all, values_all)
        second_part = guarded_grads(halves[1], start_row, block_rows, keys_all, values_all)
        return (
            (running[0] + first_part[0], running[1] + second_part[0]),
            (first_part[1] + second_part[1], first_part[2] + second_part[2]),
        )

    query_parts, (key_terms, value_terms) = lax.scan(
        soft_block_step, (zero_query, zero_query), jnp.arange(block_count)
    )
    key_grad, value_grad = (
        lax.psum_scatter(
            key_terms.reshape(key_count, key_width).astype(jnp.bfloat16),
            "ctx",
            scatter_dimension=0,
            tiled=True,
        ).astype(jnp.float32),
        lax.psum_scatter(
            value_terms.reshape(key_count, key_width).astype(jnp.bfloat16),
            "ctx",
            scatter_dimension=0,
            tiled=True,
        ).astype(jnp.float32),
    )
    query_halves = [
        query_parts[half_index]
        .transpose(2, 0, 1, 3)
        .reshape(half_rows, query_width)
        .astype(jnp.bfloat16)
        for half_index in range(2)
    ]
    return (
        out_halves,
        query_halves,
        key_grad.astype(jnp.bfloat16),
        value_grad.astype(jnp.bfloat16),
    )


def body(
    lin_query,
    lin_key,
    lin_value,
    log_decay,
    norm_gain,
    lin_gate,
    lin_grad,
    soft_query,
    soft_key,
    soft_value,
    soft_grad,
):
    lin_out, lin_query_grad, lin_key_grad, lin_value_grad, lin_gate_grad = lightning(
        lin_query, lin_key, lin_value, log_decay, norm_gain, lin_gate, lin_grad
    )
    keys_all, values_all = (
        lax.all_gather(soft_key, "ctx", axis=0, tiled=True),
        lax.all_gather(soft_value, "ctx", axis=0, tiled=True),
    )
    row_count = soft_query.shape[0]
    half_rows = row_count // 2
    ctx_index = lax.axis_index("ctx")
    starts = (ctx_index * row_count, ctx_index * row_count + half_rows)
    out_halves, query_halves, soft_key_grad, soft_value_grad = soft_attention(
        soft_query, keys_all, values_all, soft_grad, starts
    )
    second_out = out_halves[1]
    second_query = query_halves[1]
    soft_out = jnp.concatenate((out_halves[0], second_out), axis=0)
    soft_query_grad = jnp.concatenate((query_halves[0], second_query), axis=0)
    return (
        lin_out,
        lin_query_grad,
        lin_key_grad,
        lin_value_grad,
        lin_gate_grad,
        soft_out,
        soft_query_grad,
        soft_key_grad,
        soft_value_grad,
    )


def solution(mesh):
    placed = (
        P("ctx", "tp"),
        P("ctx", "tp"),
        P("ctx", "tp"),
        P("tp", "ctx"),
        P("tp"),
        P("ctx", "tp"),
        P("ctx", "tp"),
        P("ctx", "tp"),
        P("ctx", "tp"),
        P("ctx", "tp"),
        P("ctx", "tp"),
    )
    return jax.shard_map(
        body,
        mesh=mesh,
        in_specs=placed,
        out_specs=(
            P("ctx", "tp"),
            P("ctx", "tp"),
            P("ctx", "tp"),
            P("ctx", "tp"),
            P("ctx", "tp"),
            P("ctx", "tp"),
            P("ctx", "tp"),
            P("ctx", "tp"),
            P("ctx", "tp"),
        ),
        check_vma=False,
    )
```

profile of v0, /device:TPU:2, one launch (start us, length us, event | category | flops | bytes accessed | tf_op | source)
XLA Modules:
  0.0 1040.5 jit_solution(13726611066516874531)
XLA Ops:
  9.4 1.2 reduce-window.6
  11.3 2.5 convolution_convert_fusion.1
  17.5 78.3 %all-reduce = bf16[128]{0:T(256)(128)(2,1)S(1)} all-reduce(bf16[128]{0:T(256)(128)(2,1)S(1)} %dynamic-update-slice), channel_id=2, replica_groups=mesh['ctx'=32,'tp'=8] {'ctx'}, use_global_device_ids=true, to_apply=%add | all-reduce | flops 128 | bytes 512
  97.2 72.2 %all-gather.8.cloned.1.call-done = bf16[8192,128]{1,0:T(8,128)(2,1)} async-done(((bf16[256,128]{1,0:T(8,128)(2,1)}), bf16[8192,128]{1,0:T(8,128)(2,1)}) %all-gather.8.cloned.1.call-update) | async-done | bytes 2097168 | tf_op jit(solution)/shard_map/all_gather | solution.py:314
  169.4 23.8 %while.76 = (s32[]{:T(128)}, f32[1,4,128]{2,1,0:T(4,128)S(1)}, f32[1,4,128]{2,1,0:T(4,128)S(1)}, f32[1,4,128,128]{3,2,1,0:T(8,128)S(1)}, s32[16]{0:T(128)S(1)}, ...) while((s32[]{:T(128)}, f32[1,4,128]{2,1,0:T(4,128)S(1)}, ...), condition=%wide.region_21.22_spmd.clone, body=%wide.region_16.21_spmd.clone.sunk | while | flops 136775808 | bytes 4364621 | solution.py:163
  170.7 3.1 conditional.13
  170.9 1.2 select_reduce_fusion.1
  172.1 1.4 fusion.27
  193.5 23.8 %while.75 = (s32[]{:T(128)}, f32[1,4,128]{2,1,0:T(4,128)S(1)}, f32[1,4,128]{2,1,0:T(4,128)S(1)}, f32[1,4,128,128]{3,2,1,0:T(8,128)S(1)}, s32[16]{0:T(128)S(1)}, ...) while((s32[]{:T(128)}, f32[1,4,128]{2,1,0:T(4,128)S(1)}, ...), condition=%wide.region_15.16_spmd.clone, body=%wide.region_10.15_spmd.clone.sunk | while | flops 136775808 | bytes 4364621 | solution.py:163
  194.8 3.1 conditional.12
  195.0 1.2 select_reduce_fusion
  196.2 1.4 fusion.9
  218.5 33.2 %all-gather.12.cloned.1.call-done = bf16[128,128,128]{2,1,0:T(8,128)(2,1)} async-done(((bf16[4,128,128]{2,1,0:T(8,128)(2,1)}), bf16[128,128,128]{2,1,0:T(8,128)(2,1)}) %all-gather.12.cloned.1.call-update) | async-done | bytes 4194320 | tf_op jit(solution)/shard_map/all_gather | solution.py:19
  253.5 10.1 psum.14
  264.6 12.4 %psum.15 = f32[256]{0:T(256)S(1)} all-reduce(f32[256]{0:T(256)S(1)} %multiply_reduce_fusion), channel_id=1, replica_groups=mesh['ctx'=32,'tp'=8] {'tp'}, use_global_device_ids=true, to_apply=%region_7.8 | all-reduce | flops 256 | bytes 2048 | tf_op jit(solution)/shard_map/psum | solution.py:75
  277.1 1.8 fusion.108
  279.1 1.1 convolution_convert_fusion
  280.9 66.7 %while.77 = (s32[]{:T(128)}, f32[1,4,128,128]{3,2,1,0:T(8,128)S(1)}, f32[1,4,128,128]{3,2,1,0:T(8,128)S(1)}, bf16[16,512,1,128]{3,1,2,0:T(8,128)(2,1)}, bf16[16,...) while((s32[]{:T(128)}, ...), condition=%wide.region_29.30_spmd.clone, body=%wide.region_24.29_spmd.clone.sunk | while | flops 675546368 | bytes 16274487 | solution.py:265
  280.9 1.2 dynamic_slice.124
  282.8 4.6 conditional.15
  283.0 1.3 fusion.49
  284.3 1.2 fusion.51
  285.8 1.2 fusion.54
  287.9 5.1 conditional.14
  288.7 1.3 fusion.75
  289.9 1.2 fusion.77
  291.5 1.2 fusion.80
  294.0 1.3 dynamic_slice.124
  297.5 1.3 dynamic_slice.124
  301.2 1.3 dynamic_slice.124
  304.7 1.3 dynamic_slice.124
  308.3 1.3 dynamic_slice.124
  311.9 1.3 dynamic_slice.124
  315.5 1.3 dynamic_slice.124
  319.0 1.3 dynamic_slice.124
  322.6 1.3 dynamic_slice.124
  326.2 1.3 dynamic_slice.124
  329.8 1.3 dynamic_slice.124
  333.3 1.3 dynamic_slice.124
  336.9 1.3 dynamic_slice.124
  340.5 1.3 dynamic_slice.124
  344.1 1.3 dynamic_slice.124
  352.8 117.0 %all-gather.14.cloned.1.call-done = bf16[128,128,128]{2,1,0:T(8,128)(2,1)} async-done(((bf16[4,128,128]{2,1,0:T(8,128)(2,1)}), bf16[128,128,128]{2,1,0:T(8,128)(2,1)}) %all-gather.14.cloned.1.call-update) | async-done | bytes 4194320 | tf_op jit(solution)/shard_map/all_gather | solution.py:19
  469.8 53.2 %while.74 = (s32[]{:T(128)}, f32[4,128,128]{2,1,0:T(8,128)S(1)}, s32[]{:T(128)}, bf16[32,4]{1,0:T(8,128)(2,1)}, bf16[32,4,128,128]{3,2,1,0:T(8,128)(2,1)}, /*index=5*/s32[]{:T(128)}, s32[]{:T(128)}, s32[]{:T(128)}, s32[]{:T(128)}) while((s32[]{:T(128)}, f32[4,128,128]{2,1,0:T(8,128)S(1)}, s32[]{:T(128)}, bf16[32,4]{1,0:T(8,128)(2,1)}, ...), condition=%wide.region_9.10_spmd, body=%wide.region_8.9_spmd.sunk | while | flops 196618 | bytes 655547 | solution.py:34
  472.1 1.0 convert_add_fusion.5
  473.8 1.0 convert_add_fusion.5
  526.2 288.2 %reduce-scatter.3.cloned.1.call-done = bf16[256,128]{1,0:T(8,128)(2,1)} async-done(((bf16[8192,128]{1,0:T(8,128)(2,1)}), bf16[256,128]{1,0:T(8,128)(2,1)}) %reduce-scatter.3.cloned.1.call-update) | async-done | bytes 65552 | tf_op jit(solution)/shard_map/reduce_scatter | solution.py:269
  814.4 219.3 %reduce-scatter.5.cloned.1.call-done = bf16[256,128]{1,0:T(8,128)(2,1)} async-done(((bf16[8192,128]{1,0:T(8,128)(2,1)}), bf16[256,128]{1,0:T(8,128)(2,1)}) %reduce-scatter.5.cloned.1.call-update) | async-done | bytes 65552 | tf_op jit(solution)/shard_map/reduce_scatter | solution.py:275
  (491 shorter events, 120.7 us)
Async XLA Ops:
  7.2 4.1 copy-start
  7.2 8.2 copy-start.11
  7.2 90.0 %all-gather.10.cloned.1.call-start = ((), (), s32[]{:S(2)}) async-start(), calls=%async_computation.3 | async-start | bytes 2162688 | tf_op jit(solution)/shard_map/all_gather | solution.py:315
  7.9 161.4 %all-gather.8.cloned.1.call-start = ((), (), s32[]{:S(2)}) async-start(), calls=%async_computation.2 | async-start | bytes 2162688 | tf_op jit(solution)/shard_map/all_gather | solution.py:314
  8.7 243.0 %all-gather.12.cloned.1.call-start = ((), (), s32[]{:S(2)}) async-start(), calls=%async_computation.6 | async-start | bytes 4325376 | tf_op jit(solution)/shard_map/all_gather | solution.py:19
  11.0 85.6 %copy-start.15 = (f32[1,4,2,128]{3,1,2,0:T(4,128)}, f32[1,4,2,128]{3,1,2,0:T(4,128)S(1)}, u32[]{:S(2)}) copy-start(f32[1,4,2,128]{3,1,2,0:T(4,128)S(1)} %copy.216) | copy-start | bytes 12292
  11.0 4.9 copy-start.17
  11.3 85.2 %copy-start.12 = (bf16[256,512]{1,0:T(8,128)(2,1)S(1)}, bf16[256,512]{1,0:T(8,128)(2,1)}, u32[]{:S(2)}) copy-start(bf16[256,512]{1,0:T(8,128)(2,1)} %param.29) | copy-start | bytes 786436
  13.7 82.9 %copy-start.9 = (bf16[256,512]{1,0:T(8,128)(2,1)S(1)}, bf16[256,512]{1,0:T(8,128)(2,1)}, u32[]{:S(2)}) copy-start(bf16[256,512]{1,0:T(8,128)(2,1)} %param.30) | copy-start | bytes 786436
  13.8 456.0 %all-gather.14.cloned.1.call-start = ((), (), s32[]{:S(2)}) async-start(), calls=%async_computation.7 | async-start | bytes 4325376 | tf_op jit(solution)/shard_map/all_gather | solution.py:19
  96.6 72.8 %copy-start.13 = (pred[256,256]{1,0:T(8,128)(4,1)}, pred[256,256]{1,0:T(8,128)(4,1)S(1)}, u32[]{:S(2)}) copy-start(pred[256,256]{1,0:T(8,128)(4,1)S(1)} %iota_compare_fusion) | copy-start | bytes 196612
  97.2 155.2 %copy-start.3 = (bf16[4,256,256]{2,1,0:T(8,128)(2,1)}, bf16[4,256,256]{2,1,0:T(8,128)(2,1)S(1)}, u32[]{:S(2)}) copy-start(bf16[4,256,256]{2,1,0:T(8,128)(2,1)S(1)} %fusion.96) | copy-start | bytes 1572868
  217.6 34.1 %copy-start.5 = (bf16[128,512]{1,0:T(8,128)(2,1)}, bf16[128,512]{1,0:T(8,128)(2,1)S(1)}, u32[]{:S(2)}) copy-start(bf16[128,512]{1,0:T(8,128)(2,1)S(1)} %get-tuple-element.852) | copy-start | bytes 393220
  251.7 11.9 %copy-start.7 = (bf16[256,512]{1,0:T(8,128)(2,1)S(1)}, bf16[256,512]{1,0:T(8,128)(2,1)}, u32[]{:S(2)}) copy-start(bf16[256,512]{1,0:T(8,128)(2,1)} %param.35) | copy-start | bytes 786436
  251.7 11.9 %copy-start.8 = (bf16[256,512]{1,0:T(8,128)(2,1)S(1)}, bf16[256,512]{1,0:T(8,128)(2,1)}, u32[]{:S(2)}) copy-start(bf16[256,512]{1,0:T(8,128)(2,1)} %param.34) | copy-start | bytes 786436
  279.0 1.8 copy-start.1
  280.1 534.2 %reduce-scatter.3.cloned.1.call-start = ((), (), s32[]{:S(2)}) async-start(), calls=%async_computation.4 | async-start | bytes 2162688 | tf_op jit(solution)/shard_map/reduce_scatter | solution.py:269
  347.6 1.0 copy-start.6
  347.7 686.0 %reduce-scatter.5.cloned.1.call-start = ((), (), s32[]{:S(2)}) async-start(), calls=%async_computation.5 | async-start | bytes 2162688 | tf_op jit(solution)/shard_map/reduce_scatter | solution.py:275
  347.7 2.3 copy-start.2
  348.2 2.4 copy-start.14
  348.2 2.4 copy-start.16
  349.3 1.8 copy-start.10
  350.7 1.7 copy-start.4
Sparse Core Ops, SparseCore 0:
  10.6 80.7 all-gather.9
  94.0 75.3 all-gather.7
  172.5 79.0 all-gather.11
  280.3 189.4 all-gather.13
  474.1 340.2 reduce-scatter.2
  819.1 214.4 reduce-scatter.4
where the time goes:
time: 1050 us; the launch traced here: 1040 us
  waiting for transfers between devices  732 us (70%)
  blocking collectives  101 us (10%)
  other arithmetic  75.7 us (7%)
  local copies, waits for them, and re-layouts  58.3 us (6%)
  loops' own time  35.3 us (3%)
  matrix products  22.8 us (2%)
  between operations  15.4 us (1%)
    reduce_scatter x1, waiting for transfers between devices, soft_attention(): lax.psum_scatter(key_terms.reshape(key_count, key_width).astype(jnp.bfloa...  288 us
    reduce_scatter x1, waiting for transfers between devices, soft_attention(): lax.psum_scatter(value_terms.reshape(key_count, key_width).astype(jnp.bfl...  219 us
    all_gather x2, waiting for transfers between devices, carried_in(): lax.all_gather(a.astype(kind), axis)  150 us
    unnamed x1, blocking collectives  78.3 us
    all_gather x1, waiting for transfers between devices, body(): lax.all_gather(soft_key, 'ctx', axis=0, tiled=True)  72.2 us
    dynamic_slice x48, local copies, waits for them, and re-layouts, half_forward(): final_state, _ = lax.scan(half_block_step, initial, jnp.arange(block_count))  38.8 us
    add x31, other arithmetic, combine_state(): jnp.exp(later[0])[:, None, None] * earlier[1] + later[1]  31.5 us
    another operation x2, loops' own time, half_forward(): final_state, _ = lax.scan(half_block_step, initial, jnp.arange(block_count))  22.1 us
  transfers between devices with their start and end apart: 6, of which 5 were waited for; matrix products, arithmetic and copies ran while one was open for 15% of the time, Pallas kernels for 0%

commit v1 on v0

v1 whole, which is shorter than its diff:
```python
import math

import jax
import jax.numpy as jnp
from jax import lax
from jax.experimental import pallas as pl
from jax.experimental.pallas import tpu as pltpu
from jax.sharding import PartitionSpec as P

DH = 128
HEADS = 4
TOK = 256
NY = 4
NZ = 8
NT = 8
ROW = NY * TOK
WIDTH = 4096
MSG = DH + 16
F32 = jnp.float32
BF16 = jnp.bfloat16
MESH = pl.DeviceIdType.MESH
SCALE = DH ** (-0.5)
LOG2E = math.log2(math.e)
EXP_SCALE = SCALE * LOG2E
NEG = -1e30
EXACT = lax.Precision.HIGHEST


def nn(a, b, precision=None):
    return lax.dot_general(a, b, (((1,), (0,)), ((), ())), precision=precision, preferred_element_type=F32)


def nt(a, b, precision=None):
    return lax.dot_general(a, b, (((1,), (1,)), ((), ())), precision=precision, preferred_element_type=F32)


def tn(a, b, precision=None):
    return lax.dot_general(a, b, (((0,), (0,)), ((), ())), precision=precision, preferred_element_type=F32)


def cols(h):
    return slice(h * DH, (h + 1) * DH)


def kernel(
    lq, lk, lv, ld, gain, gate, lgrad, sq, sk, sv, so,
    lin_out, dlq, dlk, dlv, dgate, sout, dsq, dsk, dsv,
    kall, vall, q_t, g_t, v_t, k_t, peak, total, out_t, log_s, delta_s, dq_t, dk_acc, dv_acc,
    dks, dkr, dvs, dvy, dv_own, dvz, dvr, dky,
    decay, weights, gweights, tail_s, lead_s, att, gr_att, msg, st, pre, lead_tot, rmsg, rst, cmsg, car, tps, tpr,
    ky_s, ky_r, ks_s, kr_r, vs_s, vr_r, vy_s, vy_r, p1_s, p1_r, p2_s, p2_r, p3_s, p3_r, tp_s, tp_r,
    dk_s, dk_r, dv_s, dv_r, dvy_s, dvy_r, dky_s, dky_r,
):
    ctx = lax.axis_index("ctx")
    tp = lax.axis_index("tp")
    z = lax.div(ctx, NY)
    y = lax.rem(ctx, NY)

    def at_ctx(zz, yy):
        return {"ctx": zz * NY + yy}

    def y_peer(j):
        return lax.rem(y + j, NY)

    def y_from(j):
        return lax.rem(y + NY - j, NY)

    def copy(src, dst, s, r, device):
        return pltpu.make_async_remote_copy(
            src_ref=src, dst_ref=dst, send_sem=s, recv_sem=r, device_id=device, device_id_type=MESH
        )

    neighbour = at_ctx(z, y_peer(1))

    def arrived(dst, r, s):
        copy(dst, dst, s, r, neighbour).wait_recv()

    def sent(src, s, r):
        copy(src, src, s, r, neighbour).wait_send()

    barrier = pltpu.get_barrier_semaphore()
    for j in range(1, NY):
        pl.semaphore_signal(barrier, inc=1, device_id=at_ctx(z, y_peer(j)), device_id_type=MESH)
    for j in range(1, NZ):
        pl.semaphore_signal(barrier, inc=1, device_id=at_ctx(lax.rem(z + j, NZ), y), device_id_type=MESH)
    for j in range(1, NT):
        pl.semaphore_signal(barrier, inc=1, device_id={"tp": lax.rem(tp + j, NT)}, device_id_type=MESH)
    pl.semaphore_wait(barrier, NY + NZ + NT - 3)

    def block_at(zz, yy):
        return pl.ds(pl.multiple_of((zz * NY + yy) * TOK, TOK), TOK)

    def row_at(zz):
        return pl.ds(pl.multiple_of(zz * ROW, ROW), ROW)

    def key_to_peer(j):
        return copy(sk, kall.at[block_at(z, y)], ky_s.at[j - 1], ky_r.at[j - 1], at_ctx(z, y_peer(j)))

    def value_to_peer(d, j):
        ref = vall.at[block_at(z - d, y)]
        at = d * 3 + j - 1
        return copy(ref, ref, vy_s.at[at], vy_r.at[at], at_ctx(z, y_peer(j)))

    def row_to(d, to_z, to_d, at):
        ref = kall.at[row_at(z - d)]
        return copy(ref, ref, ks_s.at[at], kr_r.at[to_d], at_ctx(to_z, y))

    def value_to(d, to_z, to_d, at):
        ref = vall.at[block_at(z - d, y)]
        return copy(ref, ref, vs_s.at[at], vr_r.at[to_d], at_ctx(to_z, y))

    up = z < NZ - 1
    low = z <= 2
    last = NZ - 1

    def fetch(d):
        @pl.when(z >= d)
        def _():
            arrived(vall.at[block_at(z - d, y)], vr_r.at[d], vs_s.at[d])

            @pl.when((d <= 3) & up)
            def _():
                value_to(d, z + 1, d + 1, d).start()

            @pl.when(d >= 6)
            def _():
                value_to(d, z - 1, d - 1, d).start()

            for j in range(1, NY):
                value_to_peer(d, j).start()
            arrived(kall.at[row_at(z - d)], kr_r.at[d], ks_s.at[d])

            @pl.when((d <= 3) & up)
            def _():
                row_to(d, z + 1, d + 1, d).start()

            @pl.when(d >= 6)
            def _():
                row_to(d, z - 1, d - 1, d).start()

    def peer_values(d):
        for j in range(1, NY):
            at = d * 3 + j - 1
            arrived(vall.at[block_at(z - d, y_from(j))], vy_r.at[at], vy_s.at[at])

    kall[block_at(z, y), :] = sk[...]
    vall[block_at(z, y), :] = sv[...]
    for j in range(1, NY):
        key_to_peer(j).start()

    @pl.when(up)
    def _():
        value_to(0, z + 1, 1, 0).start()

    @pl.when(low)
    def _():
        value_to(0, last, last - z, 4).start()

    for j in range(1, NY):
        value_to_peer(0, j).start()

    for h in range(HEADS):
        q_t[h] = sq[:, cols(h)].T
        g_t[h] = so[:, cols(h)].T

    for j in range(1, NY):
        arrived(kall.at[block_at(z, y_from(j))], ky_r.at[j - 1], ky_s.at[j - 1])

    @pl.when(up)
    def _():
        row_to(0, z + 1, 1, 0).start()

    @pl.when(low)
    def _():
        row_to(0, last, last - z, 4).start()

    def coded(tot):
        first = tot.astype(BF16).astype(F32)
        second = (tot - first).astype(BF16).astype(F32)
        third = (tot - first - second).astype(BF16).astype(F32)
        r = lax.broadcasted_iota(jnp.int32, (16, DH), 0)
        rows = jnp.where(r == 0, first, jnp.where(r == 1, second, jnp.where(r == 2, third, 0.0)))
        return rows.astype(BF16)

    def decoded(rows):
        return jnp.sum(rows.astype(F32), axis=0, keepdims=True)

    def state_to_peer(k, j):
        at = k * 3 + j - 1
        return copy(msg.at[k, y_peer(j)], st.at[k, y], p1_s.at[at], p1_r.at[at], at_ctx(z, y_peer(j)))

    def total_to(k, zz):
        return copy(rmsg.at[k], rst.at[k, z], p2_s.at[k * NZ + zz], p2_r.at[k * NZ + z], at_ctx(zz, y))

    def carried_to_peer(k, j):
        at = k * 3 + j - 1
        return copy(cmsg.at[k, y_peer(j)], car.at[k, y], p3_s.at[at], p3_r.at[at], at_ctx(z, y_peer(j)))

    def send_states(k):
        st[k, y] = msg[k, y]
        for j in range(1, NY):
            state_to_peer(k, j).start()

    def z_targets(k):
        return (z + 1, NZ) if k == 0 else (0, z)

    def join_row(k):
        for j in range(1, NY):
            at = k * 3 + j - 1
            arrived(st.at[k, y_from(j)], p1_r.at[at], p1_s.at[at])
        order = range(NY) if k == 0 else range(NY - 1, -1, -1)
        state = jnp.zeros((DH, DH), F32)
        so_far = jnp.zeros((1, DH), F32)
        for i in order:
            pre[i] = state
            lead_tot[i] = so_far
            tot = decoded(st[k, i, DH:, :])
            state = jnp.exp(tot) * state + st[k, i, :DH, :].astype(F32)
            so_far = so_far + tot
        rmsg[k, :DH, :] = state.astype(BF16)
        rmsg[k, DH:, :] = coded(so_far)

        def one(zz, c):
            total_to(k, zz).start()
            return c

        lax.fori_loop(*z_targets(k), one, 0)

    def join_all(k):
        def one(i, state):
            zz = i if k == 0 else NZ - 1 - i
            at = k * NZ + zz
            arrived(rst.at[k, zz], p2_r.at[at], p2_s.at[at])
            return jnp.exp(decoded(rst[k, zz, DH:, :])) * state + rst[k, zz, :DH, :].astype(F32)

        state = lax.fori_loop(0, z if k == 0 else NZ - 1 - z, one, jnp.zeros((DH, DH), F32))
        for i in range(NY):
            cmsg[k, i] = (pre[i] + jnp.exp(lead_tot[i]) * state).astype(BF16)
        car[k, y] = cmsg[k, y]
        for j in range(1, NY):
            carried_to_peer(k, j).start()

    def take_carried(k):
        for j in range(1, NY):
            at = k * 3 + j - 1
            arrived(car.at[k, y_from(j)], p3_r.at[at], p3_s.at[at])

    logs = jnp.concatenate([ld[...], jnp.zeros((8 - HEADS, TOK), F32)], axis=0)
    earlier = lax.broadcasted_iota(jnp.int32, (TOK, TOK), 0)
    later = lax.broadcasted_iota(jnp.int32, (TOK, TOK), 1)
    log_rows = nn(logs, (earlier <= later).astype(F32), EXACT)
    log_cols = nt((later <= earlier).astype(F32), logs, EXACT)
    causal = earlier >= later
    for h in range(HEADS):
        col = log_cols[:, h : h + 1]
        row = log_rows[h : h + 1, :]
        tot = log_rows[h : h + 1, TOK - 1 :]
        dec = jnp.exp(jnp.where(causal, col - row, NEG))
        decay[h] = dec
        tail = jnp.broadcast_to(jnp.exp(tot - col), (TOK, DH))
        tail_s[h] = tail
        lead_s[h] = jnp.broadcast_to(jnp.exp(col), (TOK, DH))
        kk = lk[:, cols(h)]
        weights[h] = (nt(lq[:, cols(h)], kk) * dec).astype(BF16)
        msg[0, h, :DH, :] = tn((kk.astype(F32) * tail).astype(BF16), lv[:, cols(h)]).astype(BF16)
        code = coded(jnp.broadcast_to(tot, (1, DH)))
        msg[0, h, DH:, :] = code
        msg[1, h, DH:, :] = code
    send_states(0)

    def gated(h):
        sig = jax.nn.sigmoid(gate[:, cols(h)].astype(F32))
        return sig, gain[:, cols(h)], lgrad[:, cols(h)].astype(F32)

    def sums_to(j):
        return copy(tps, tpr.at[j], tp_s.at[j - 1], tp_r.at[j - 1], {"tp": lax.rem(tp + j, NT)})

    def attend():
        take_carried(0)
        squares = jnp.zeros((TOK, DH), F32)
        cross = jnp.zeros((TOK, DH), F32)
        for h in range(HEADS):
            a = nn(weights[h], lv[:, cols(h)]) + lead_s[h] * nn(lq[:, cols(h)], car[0, h])
            att[:, cols(h)] = a
            sig, gn, gr = gated(h)
            squares = squares + a * a
            cross = cross + gr * gn * sig * a
        ones = jnp.ones((8, DH), F32)
        tps[0:8, :] = nt(ones, squares, EXACT)
        tps[8:16, :] = nt(ones, cross, EXACT)
        for j in range(1, NT):
            sums_to(j).start()

    def norm_and_grad():
        tot = tps[...]
        for j in range(1, NT):
            arrived(tpr.at[j], tp_r.at[j - 1], tp_s.at[j - 1])
            tot = tot + tpr[j]
        rms_row = lax.rsqrt(tot[0:8] / WIDTH + 1e-05)
        mean_row = rms_row * tot[8:16] / WIDTH
        eye = (earlier == later).astype(F32)
        rms = nt(eye, rms_row, EXACT)[:, 0:1]
        mean = nt(eye, mean_row, EXACT)[:, 0:1]
        for h in range(HEADS):
            sig, gn, gr = gated(h)
            normed = att[:, cols(h)] * rms
            by_gain = normed * gn * sig
            lin_out[:, cols(h)] = by_gain.astype(BF16)
            dgate[:, cols(h)] = (gr * by_gain * (1.0 - sig)).astype(BF16)
            da = (rms * (gr * gn * sig - normed * mean)).astype(BF16)
            gr_att[:, cols(h)] = da
            gweights[h] = (nt(da, lv[:, cols(h)]) * decay[h]).astype(BF16)
            msg[1, h, :DH, :] = tn((lq[:, cols(h)].astype(F32) * lead_s[h]).astype(BF16), da).astype(BF16)
        send_states(1)

    def lin_grads():
        take_carried(1)
        for h in range(HEADS):
            da = gr_att[:, cols(h)]
            kk = lk[:, cols(h)]
            dlq[:, cols(h)] = (nn(gweights[h], kk) + lead_s[h] * nt(da, car[0, h])).astype(BF16)
            dlk[:, cols(h)] = (
                tn(gweights[h], lq[:, cols(h)]) + tail_s[h] * nt(lv[:, cols(h)], car[1, h])
            ).astype(BF16)
            dlv[:, cols(h)] = (tn(weights[h], da) + tail_s[h] * nn(kk, car[1, h])).astype(BF16)

    def fwd_tile(h, keys, values_t, key_start):
        s = nn(keys, q_t[h])
        if key_start is not None:
            key_at = key_start + lax.broadcasted_iota(jnp.int32, s.shape, 0)
            query_at = y * TOK + lax.broadcasted_iota(jnp.int32, s.shape, 1)
            s = jnp.where(key_at <= query_at, s, NEG)
        old = peak[h]
        new = jnp.maximum(old, jnp.max(s, axis=0, keepdims=True))
        shrink = jnp.exp2((old - new) * EXP_SCALE)
        p = jnp.exp2((s - new) * EXP_SCALE)
        peak[h] = new
        total[h] = total[h] * shrink + jnp.sum(p, axis=0, keepdims=True)
        out_t[h] = out_t[h] * shrink + nn(values_t, p.astype(BF16))

    def fwd_row(d):
        rows = row_at(z - d)
        v_t[...] = vall[rows, :].T

        def head(h, c):
            fwd_tile(h, kall[rows, :], v_t[...], None)
            return c

        lax.fori_loop(0, HEADS, head, 0)

    def fwd_diagonal():
        for h in range(HEADS):
            peak[h] = jnp.full((1, TOK), NEG, F32)
            total[h] = jnp.zeros((1, TOK), F32)
            out_t[h] = jnp.zeros((DH, TOK), F32)

        def one(i, c):
            yy = y - i
            rows = block_at(z, yy)
            v_t[:, :TOK] = vall[rows, :].T

            def head(h, c):
                fwd_tile(h, kall[rows, :], v_t[:, :TOK], yy * TOK)
                return c

            return lax.fori_loop(0, HEADS, head, c)

        lax.fori_loop(0, y + 1, one, 0)

    def finish_forward():
        for h in range(HEADS):
            o = (out_t[h] / total[h]).astype(BF16)
            sout[:, cols(h)] = o.T
            delta_s[h] = jnp.sum(g_t[h].astype(F32) * o.astype(F32), axis=0, keepdims=True)
            log_s[h] = peak[h] * EXP_SCALE + jnp.log(total[h]) * LOG2E
            dq_t[h] = jnp.zeros((DH, TOK), F32)

    def bwd_tile(h, keys, values, keys_t, key_start):
        s = nn(keys, q_t[h])
        p = jnp.exp2(s * EXP_SCALE - log_s[h])
        if key_start is not None:
            key_at = key_start + lax.broadcasted_iota(jnp.int32, s.shape, 0)
            query_at = y * TOK + lax.broadcasted_iota(jnp.int32, s.shape, 1)
            p = jnp.where(key_at <= query_at, p, 0.0)
        dp = nn(values, g_t[h])
        ds = (p * (dp - delta_s[h])).astype(BF16)
        dq_t[h] = dq_t[h] + nn(keys_t, ds)
        at = pl.ds(pl.multiple_of(h * DH, DH), DH)
        return nn(ds, sq[:, at]), nn(p.astype(BF16), so[:, at])

    def bwd_row(d):
        rows = row_at(z - d)
        k_t[...] = kall[rows, :].T
        dk_acc[...] = jnp.zeros((ROW, DH), F32)
        dv_acc[...] = jnp.zeros((ROW, DH), F32)

        def head(h, c):
            dk, dv = bwd_tile(h, kall[rows, :], vall[rows, :], k_t[...], None)
            dk_acc[...] = dk_acc[...] + dk
            dv_acc[...] = dv_acc[...] + dv
            return c

        lax.fori_loop(0, HEADS, head, 0)

    def local_block(yy):
        return pl.ds(pl.multiple_of(yy * TOK, TOK), TOK)

    def bwd_diagonal():
        dk_acc[...] = jnp.zeros((ROW, DH), F32)
        dv_acc[...] = jnp.zeros((ROW, DH), F32)

        def one(yy, c):
            rows = block_at(z, yy)
            own = local_block(yy)
            k_t[:, :TOK] = kall[rows, :].T

            def head(h, c):
                dk, dv = bwd_tile(h, kall[rows, :], vall[rows, :], k_t[:, :TOK], yy * TOK)
                dk_acc[own, :] = dk_acc[own, :] + dk
                dv_acc[own, :] = dv_acc[own, :] + dv
                return c

            return lax.fori_loop(0, HEADS, head, c)

        lax.fori_loop(0, y + 1, one, 0)

    def target(d):
        near = d <= 4
        to_z = jnp.where(near, z - 1, jnp.where(up, z + 1, z - d))
        slot = jnp.where(near, d - 1, jnp.where(up, d + 1, 4))
        return to_z, slot

    def has_incoming(d):
        return ((d <= 3) & up) | (d >= 6)

    def dk_copy(d):
        to_z, slot = target(d)
        return copy(dks.at[d], dkr.at[slot], dk_s.at[d], dk_r.at[slot], at_ctx(to_z, y))

    def dv_copy(d):
        to_z, slot = target(d)
        return copy(dvz.at[d], dvr.at[slot], dv_s.at[d], dv_r.at[slot], at_ctx(to_z, y))

    def dv_to_peer(d, j):
        at = d * 3 + j - 1
        src = dvs.at[d, local_block(y_peer(j))]
        return copy(src, dvy.at[d, j], dvy_s.at[at], dvy_r.at[at], at_ctx(z, y_peer(j)))

    def dk_to_peer(j):
        src = dks.at[0, local_block(y_peer(j))]
        return copy(src, dky.at[j], dky_s.at[j - 1], dky_r.at[j - 1], at_ctx(z, y_peer(j)))

    def spread_dv(d):
        dvs[d] = dv_acc[...].astype(BF16)
        dv_own[d] = dv_acc[local_block(y), :]
        for j in range(1, NY):
            dv_to_peer(d, j).start()

    def own_dv(d):
        acc = dv_own[d]
        for j in range(1, NY):
            at = d * 3 + j - 1
            arrived(dvy.at[d, j], dvy_r.at[at], dvy_s.at[at])
            acc = acc + dvy[d, j].astype(F32)
        return acc

    def add_incoming(acc, slots, sems, others, slot):
        arrived(slots.at[slot], sems.at[slot], others.at[slot])
        acc[...] = acc[...] + slots[slot].astype(F32)

    def pass_dk(d):
        @pl.when(has_incoming(d))
        def _():
            add_incoming(dk_acc, dkr, dk_r, dk_s, d)

        dks[d] = dk_acc[...].astype(BF16)
        dk_copy(d).start()

    part = dv_acc.at[pl.ds(0, TOK)]

    def pass_dv(d):
        @pl.when(z >= d)
        def _():
            part[...] = own_dv(d)

            @pl.when(has_incoming(d))
            def _():
                add_incoming(part, dvr, dv_r, dv_s, d)

            dvz[d] = part[...].astype(BF16)
            dv_copy(d).start()

    def fwd_order(t):
        return jnp.where(lax.rem(t, 2) == 1, lax.div(t + 1, 2), NZ - lax.div(t, 2))

    def bwd_order(t):
        return jnp.where(lax.rem(t, 2) == 0, 4 - lax.div(t, 2), 5 + lax.div(t - 1, 2))

    fetch(1)
    peer_values(0)
    fwd_diagonal()

    events = (
        lambda: join_row(0),
        lambda: join_all(0),
        attend,
        norm_and_grad,
        lambda: join_row(1),
        lambda: join_all(1),
        lin_grads,
    )

    def fwd_step(t, c):
        d = fwd_order(t)

        @pl.when(t < NZ - 1)
        def _():
            fetch(fwd_order(t + 1))

        @pl.when(z >= d)
        def _():
            peer_values(d)
            fwd_row(d)

        for i, event in enumerate(events):
            pl.when(t == i + 1)(event)
        return c

    lax.fori_loop(1, NZ, fwd_step, 0)
    finish_forward()

    def bwd_step(t, c):
        d = bwd_order(t)

        @pl.when(z >= d)
        def _():
            bwd_row(d)
            spread_dv(d)
            pass_dk(d)

        @pl.when(t > 0)
        def _():
            pass_dv(bwd_order(t - 1))

        return c

    lax.fori_loop(0, NZ - 1, bwd_step, 0)
    bwd_diagonal()
    spread_dv(0)

    @pl.when(up)
    def _():
        add_incoming(dk_acc, dkr, dk_r, dk_s, 0)

    @pl.when(low)
    def _():
        add_incoming(dk_acc, dkr, dk_r, dk_s, 4)

    dks[0] = dk_acc[...].astype(BF16)
    for j in range(1, NY):
        dk_to_peer(j).start()
    pass_dv(1)
    for h in range(HEADS):
        dsq[:, cols(h)] = (dq_t[h] * SCALE).T.astype(BF16)
    part[...] = own_dv(0)

    @pl.when(up)
    def _():
        add_incoming(part, dvr, dv_r, dv_s, 0)

    @pl.when(low)
    def _():
        add_incoming(part, dvr, dv_r, dv_s, 4)

    dsv[...] = part[...].astype(BF16)
    acc = dk_acc[local_block(y), :]
    for j in range(1, NY):
        arrived(dky.at[j], dky_r.at[j - 1], dky_s.at[j - 1])
        acc = acc + dky[j].astype(F32)
    dsk[...] = (acc * SCALE).astype(BF16)

    for j in range(1, NY):
        key_to_peer(j).wait_send()
        dk_to_peer(j).wait_send()
        for k in range(2):
            state_to_peer(k, j).wait_send()
            carried_to_peer(k, j).wait_send()
    for j in range(1, NT):
        sums_to(j).wait_send()
    for k in range(2):

        def gone(zz, c, k=k):
            total_to(k, zz).wait_send()
            return c

        lax.fori_loop(*z_targets(k), gone, 0)

    @pl.when(low)
    def _():
        value_to(0, last, last - z, 4).wait_send()
        row_to(0, last, last - z, 4).wait_send()

    def all_gone(d, c):
        @pl.when(z >= d)
        def _():
            @pl.when((d <= 3) & up)
            def _():
                value_to(d, z + 1, d + 1, d).wait_send()
                row_to(d, z + 1, d + 1, d).wait_send()

            @pl.when(d >= 6)
            def _():
                value_to(d, z - 1, d - 1, d).wait_send()
                row_to(d, z - 1, d - 1, d).wait_send()

            for j in range(1, NY):
                value_to_peer(d, j).wait_send()
                dv_to_peer(d, j).wait_send()

            @pl.when(d >= 1)
            def _():
                dk_copy(d).wait_send()
                dv_copy(d).wait_send()

        return c

    lax.fori_loop(0, NZ, all_gone, 0)


def body(lin_query, lin_key, lin_value, log_decay, norm_gain, lin_gate, lin_grad, soft_query, soft_key, soft_value, soft_grad):
    wide = jax.ShapeDtypeStruct((TOK, HEADS * DH), BF16)
    narrow = jax.ShapeDtypeStruct((TOK, DH), BF16)
    dma = pltpu.SemaphoreType.DMA
    vmem = pltpu.VMEM
    scratch = [
        vmem((NZ * ROW, DH), BF16),
        vmem((NZ * ROW, DH), BF16),
        vmem((HEADS, DH, TOK), BF16),
        vmem((HEADS, DH, TOK), BF16),
        vmem((DH, ROW), BF16),
        vmem((DH, ROW), BF16),
        vmem((HEADS, 1, TOK), F32),
        vmem((HEADS, 1, TOK), F32),
        vmem((HEADS, DH, TOK), F32),
        vmem((HEADS, 1, TOK), F32),
        vmem((HEADS, 1, TOK), F32),
        vmem((HEADS, DH, TOK), F32),
        vmem((ROW, DH), F32),
        vmem((ROW, DH), F32),
        vmem((NZ, ROW, DH), BF16),
        vmem((NZ, ROW, DH), BF16),
        vmem((NZ, ROW, DH), BF16),
        vmem((NZ, NY, TOK, DH), BF16),
        vmem((NZ, TOK, DH), F32),
        vmem((NZ, TOK, DH), BF16),
        vmem((NZ, TOK, DH), BF16),
        vmem((NY, TOK, DH), BF16),
        vmem((HEADS, TOK, TOK), F32),
        vmem((HEADS, TOK, TOK), BF16),
        vmem((HEADS, TOK, TOK), BF16),
        vmem((HEADS, TOK, DH), F32),
        vmem((HEADS, TOK, DH), F32),
        vmem((TOK, HEADS * DH), F32),
        vmem((TOK, HEADS * DH), BF16),
        vmem((2, HEADS, MSG, DH), BF16),
        vmem((2, NY, MSG, DH), BF16),
        vmem((NY, DH, DH), F32),
        vmem((NY, 1, DH), F32),
        vmem((2, MSG, DH), BF16),
        vmem((2, NZ, MSG, DH), BF16),
        vmem((2, NY, DH, DH), BF16),
        vmem((2, HEADS, DH, DH), BF16),
        vmem((16, TOK), F32),
        vmem((NT, 16, TOK), F32),
        dma((3,)), dma((3,)),
        dma((NZ,)), dma((NZ,)),
        dma((NZ,)), dma((NZ,)),
        dma((3 * NZ,)), dma((3 * NZ,)),
        dma((6,)), dma((6,)),
        dma((2 * NZ,)), dma((2 * NZ,)),
        dma((6,)), dma((6,)),
        dma((NT - 1,)), dma((NT - 1,)),
        dma((NZ,)), dma((NZ,)),
        dma((NZ,)), dma((NZ,)),
        dma((3 * NZ,)), dma((3 * NZ,)),
        dma((3,)), dma((3,)),
    ]
    return pl.pallas_call(
        kernel,
        out_shape=[wide] * 7 + [narrow] * 2,
        in_specs=[pl.BlockSpec(memory_space=pltpu.VMEM)] * 11,
        out_specs=[pl.BlockSpec(memory_space=pltpu.VMEM)] * 9,
        scratch_shapes=scratch,
        compiler_params=pltpu.CompilerParams(
            collective_id=0, has_side_effects=True, vmem_limit_bytes=56 * 2**20
        ),
    )(
        lin_query, lin_key, lin_value, log_decay, norm_gain.reshape(1, -1), lin_gate, lin_grad,
        soft_query, soft_key, soft_value, soft_grad,
    )


def solution(mesh):
    shared = P("ctx", "tp")
    return jax.shard_map(
        lambda *args: tuple(body(*args)),
        mesh=mesh,
        in_specs=(shared, shared, shared, P("tp", "ctx"), P("tp"), shared, shared, shared, shared, shared, shared),
        out_specs=(shared,) * 9,
        check_vma=False,
    )
```

time: 1050 us -> 126 us (0.12)
  the two profiles are of different devices: /device:TPU:2 before, /device:TPU:224 now
where the time goes in v1:
time: 126 us
  Pallas kernels  116 us (92%)
  local copies, waits for them, and re-layouts  9.28 us (7%)
    pallas_call x1, Pallas kernels, body(): pl.pallas_call(kernel, out_shape=[wide] * 7 + [narrow] * 2, in_specs=[pl....  116 us
    unnamed x25, local copies, waits for them, and re-layouts  9.28 us

profile of v1, /device:TPU:224, one launch (start us, length us, event | category | flops | bytes accessed | tf_op | source)
XLA Modules:
  0.0 125.6 jit_solution(17368677492589257323)
XLA Ops:
  0.6 115.7 %shard_map.178 = (bf16[256,512]{1,0:T(8,128)(2,1)}, bf16[256,512]{1,0:T(8,128)(2,1)}, bf16[256,512]{1,0:T(8,128)(2,1)}, bf16[256,512]{1,0:T(8,128)(2,1)}, bf16[2...) custom-call(bf16[256,512]{1,0:T(8,128)(2,1)} %lq.1, ...), custom_call_target="tpu_custom_call" | custom-call | tf_op jit(solution)/shard_map/pallas_call | solution.py:688
  116.3 0.0 copy-start.5
  116.3 1.7 %copy.29 = bf16[256,512]{1,0:T(8,128)(2,1)} copy(bf16[256,512]{1,0:T(8,128)(2,1)} %get-tuple-element.18) | data formatting | bytes 524288
  118.0 0.0 copy-done.5
  118.0 0.0 copy-start.4
  118.0 0.7 copy.30
  118.7 0.3 copy-done.4
  119.1 0.0 copy-start.3
  119.1 0.7 copy.31
  119.8 0.3 copy-done.3
  120.1 0.0 copy-start.2
  120.1 0.7 copy.32
  120.8 0.3 copy-done.2
  121.2 0.0 copy-start.1
  121.2 0.7 copy.33
  121.9 0.3 copy-done.1
  122.2 0.0 copy-start
  122.2 0.7 copy.34
  122.9 0.3 copy-done
  123.3 0.0 copy-start.7
  123.3 0.7 copy.35
  124.0 0.2 copy-done.7
  124.1 0.0 copy-start.6
  124.1 0.6 copy.36
  124.8 0.2 copy-done.6
  125.0 0.6 copy.37
Async XLA Ops:
  116.3 1.7 %copy-start.5 = (bf16[256,512]{1,0:T(8,128)(2,1)S(1)}, bf16[256,512]{1,0:T(8,128)(2,1)}, u32[]{:S(2)}) copy-start(bf16[256,512]{1,0:T(8,128)(2,1)} %get-tuple-element.19) | copy-start | bytes 786436
  118.0 1.0 copy-start.4
  119.1 1.0 copy-start.3
  120.1 1.0 copy-start.2
  121.2 1.0 copy-start.1
  122.2 1.0 copy-start
  123.3 0.9 copy-start.7
  124.1 0.9 copy-start.6

commit v2 on v1

--- a/solution.py
+++ b/solution.py
@@ -101,42 +101,60 @@
         at = d * 3 + j - 1
         return copy(ref, ref, vy_s.at[at], vy_r.at[at], at_ctx(z, y_peer(j)))
 
-    def row_to(d, to_z, to_d, at):
-        ref = kall.at[row_at(z - d)]
-        return copy(ref, ref, ks_s.at[at], kr_r.at[to_d], at_ctx(to_z, y))
-
-    def value_to(d, to_z, to_d, at):
-        ref = vall.at[block_at(z - d, y)]
-        return copy(ref, ref, vs_s.at[at], vr_r.at[to_d], at_ctx(to_z, y))
-
     up = z < NZ - 1
     low = z <= 2
-    last = NZ - 1
-
-    def fetch(d):
-        @pl.when(z >= d)
-        def _():
-            arrived(vall.at[block_at(z - d, y)], vr_r.at[d], vs_s.at[d])
-
-            @pl.when((d <= 3) & up)
+
+    def rem_z(zz):
+        return lax.rem(zz + NZ, NZ)
+
+    def half_of(zz, half):
+        return pl.ds(pl.multiple_of(zz * ROW + half * (ROW // 2), ROW // 2), ROW // 2)
+
+    def row_to(zz, to_z, step, half):
+        ref = kall.at[half_of(zz, half)]
+        at = step * 2 + half
+        return copy(ref, ref, ks_s.at[at], kr_r.at[at], at_ctx(to_z, y))
+
+    def value_to(zz, to_z, step):
+        ref = vall.at[block_at(zz, y)]
+        return copy(ref, ref, vs_s.at[step], vr_r.at[step], at_ctx(to_z, y))
+
+    def upward(s, act, more):
+        pl.when(up & more)(lambda: act(z - s, z + 1, s + 1))
+
+    def downward(s, act, more):
+        pl.when(more)(lambda: act(rem_z(z + s), rem_z(z - 1), s + 5))
+
+    def fetch_values(s):
+        @pl.when(z >= s)
+        def _():
+            arrived(vall.at[block_at(z - s, y)], vr_r.at[s], vs_s.at[s])
+            upward(s, lambda *a: value_to(*a).start(), s < 4)
+            for j in range(1, NY):
+                value_to_peer(s, j).start()
+
+        @pl.when((s <= 3) & (rem_z(z + s) <= 2))
+        def _():
+            arrived(vall.at[block_at(rem_z(z + s), y)], vr_r.at[s + 4], vs_s.at[s + 4])
+            downward(s, lambda *a: value_to(*a).start(), s < 3)
+
+            @pl.when(z + s >= NZ)
             def _():
-                value_to(d, z + 1, d + 1, d).start()
-
-            @pl.when(d >= 6)
-            def _():
-                value_to(d, z - 1, d - 1, d).start()
-
-            for j in range(1, NY):
-                value_to_peer(d, j).start()
-            arrived(kall.at[row_at(z - d)], kr_r.at[d], ks_s.at[d])
-
-            @pl.when((d <= 3) & up)
-            def _():
-                row_to(d, z + 1, d + 1, d).start()
-
-            @pl.when(d >= 6)
-            def _():
-                row_to(d, z - 1, d - 1, d).start()
+                for j in range(1, NY):
+                    value_to_peer(NZ - s, j).start()
+
+    def fetch_keys(s, half):
+        @pl.when(z >= s)
+        def _():
+            at = s * 2 + half
+            arrived(kall.at[half_of(z - s, half)], kr_r.at[at], ks_s.at[at])
+            upward(s, lambda *a: row_to(*a, half).start(), s < 4)
+
+        @pl.when((s <= 3) & (rem_z(z + s) <= 2))
+        def _():
+            at = (s + 4) * 2 + half
+            arrived(kall.at[half_of(rem_z(z + s), half)], kr_r.at[at], ks_s.at[at])
+            downward(s, lambda *a: row_to(*a, half).start(), s < 3)
 
     def peer_values(d):
         for j in range(1, NY):
@@ -148,14 +166,8 @@
     for j in range(1, NY):
         key_to_peer(j).start()
 
-    @pl.when(up)
-    def _():
-        value_to(0, z + 1, 1, 0).start()
-
-    @pl.when(low)
-    def _():
-        value_to(0, last, last - z, 4).start()
-
+    upward(0, lambda *a: value_to(*a).start(), True)
+    downward(0, lambda *a: value_to(*a).start(), low)
     for j in range(1, NY):
         value_to_peer(0, j).start()
 
@@ -166,13 +178,9 @@
     for j in range(1, NY):
         arrived(kall.at[block_at(z, y_from(j))], ky_r.at[j - 1], ky_s.at[j - 1])
 
-    @pl.when(up)
-    def _():
-        row_to(0, z + 1, 1, 0).start()
-
-    @pl.when(low)
-    def _():
-        row_to(0, last, last - z, 4).start()
+    for half in range(2):
+        upward(0, lambda *a: row_to(*a, half).start(), True)
+        downward(0, lambda *a: row_to(*a, half).start(), low)
 
     def coded(tot):
         first = tot.astype(BF16).astype(F32)
@@ -342,11 +350,8 @@
         rows = row_at(z - d)
         v_t[...] = vall[rows, :].T
 
-        def head(h, c):
+        for h in range(HEADS):
             fwd_tile(h, kall[rows, :], v_t[...], None)
-            return c
-
-        lax.fori_loop(0, HEADS, head, 0)
 
     def fwd_diagonal():
         for h in range(HEADS):
@@ -354,18 +359,10 @@
             total[h] = jnp.zeros((1, TOK), F32)
             out_t[h] = jnp.zeros((DH, TOK), F32)
 
-        def one(i, c):
-            yy = y - i
-            rows = block_at(z, yy)
-            v_t[:, :TOK] = vall[rows, :].T
-
-            def head(h, c):
-                fwd_tile(h, kall[rows, :], v_t[:, :TOK], yy * TOK)
-                return c
-
-            return lax.fori_loop(0, HEADS, head, c)
-
-        lax.fori_loop(0, y + 1, one, 0)
+        rows = row_at(z)
+        v_t[...] = vall[rows, :].T
+        for h in range(HEADS):
+            fwd_tile(h, kall[rows, :], v_t[...], 0)
 
     def finish_forward():
         for h in range(HEADS):
@@ -385,44 +382,19 @@
         dp = nn(values, g_t[h])
         ds = (p * (dp - delta_s[h])).astype(BF16)
         dq_t[h] = dq_t[h] + nn(keys_t, ds)
-        at = pl.ds(pl.multiple_of(h * DH, DH), DH)
-        return nn(ds, sq[:, at]), nn(p.astype(BF16), so[:, at])
-
-    def bwd_row(d):
+        return nn(ds, sq[:, cols(h)]), nn(p.astype(BF16), so[:, cols(h)])
+
+    def bwd_row(d, start=None):
         rows = row_at(z - d)
         k_t[...] = kall[rows, :].T
-        dk_acc[...] = jnp.zeros((ROW, DH), F32)
-        dv_acc[...] = jnp.zeros((ROW, DH), F32)
-
-        def head(h, c):
-            dk, dv = bwd_tile(h, kall[rows, :], vall[rows, :], k_t[...], None)
-            dk_acc[...] = dk_acc[...] + dk
-            dv_acc[...] = dv_acc[...] + dv
-            return c
-
-        lax.fori_loop(0, HEADS, head, 0)
+
+        for h in range(HEADS):
+            dk, dv = bwd_tile(h, kall[rows, :], vall[rows, :], k_t[...], start)
+            dk_acc[...] = dk if h == 0 else dk_acc[...] + dk
+            dv_acc[...] = dv if h == 0 else dv_acc[...] + dv
 
     def local_block(yy):
         return pl.ds(pl.multiple_of(yy * TOK, TOK), TOK)
-
-    def bwd_diagonal():
-        dk_acc[...] = jnp.zeros((ROW, DH), F32)
-        dv_acc[...] = jnp.zeros((ROW, DH), F32)
-
-        def one(yy, c):
-            rows = block_at(z, yy)
-            own = local_block(yy)
-            k_t[:, :TOK] = kall[rows, :].T
-
-            def head(h, c):
-                dk, dv = bwd_tile(h, kall[rows, :], vall[rows, :], k_t[:, :TOK], yy * TOK)
-                dk_acc[own, :] = dk_acc[own, :] + dk
-                dv_acc[own, :] = dv_acc[own, :] + dv
-                return c
-
-            return lax.fori_loop(0, HEADS, head, c)
-
-        lax.fori_loop(0, y + 1, one, 0)
 
     def target(d):
         near = d <= 4
@@ -490,43 +462,45 @@
             dvz[d] = part[...].astype(BF16)
             dv_copy(d).start()
 
-    def fwd_order(t):
-        return jnp.where(lax.rem(t, 2) == 1, lax.div(t + 1, 2), NZ - lax.div(t, 2))
-
     def bwd_order(t):
         return jnp.where(lax.rem(t, 2) == 0, 4 - lax.div(t, 2), 5 + lax.div(t - 1, 2))
 
-    fetch(1)
+    fetch_values(1)
+    fetch_keys(1, 0)
     peer_values(0)
     fwd_diagonal()
-
-    events = (
-        lambda: join_row(0),
-        lambda: join_all(0),
-        attend,
-        norm_and_grad,
-        lambda: join_row(1),
-        lambda: join_all(1),
-        lin_grads,
-    )
-
-    def fwd_step(t, c):
-        d = fwd_order(t)
-
-        @pl.when(t < NZ - 1)
-        def _():
-            fetch(fwd_order(t + 1))
-
-        @pl.when(z >= d)
-        def _():
-            peer_values(d)
-            fwd_row(d)
-
-        for i, event in enumerate(events):
-            pl.when(t == i + 1)(event)
+    fetch_keys(1, 1)
+
+    def at_steps(now, events):
+        for at, event in events:
+            pl.when(now == at)(event)
+
+    def fwd_step(s, c):
+        @pl.when(s < 4)
+        def _():
+            fetch_values(s + 1)
+            fetch_keys(s + 1, 0)
+
+        @pl.when(z >= s)
+        def _():
+            peer_values(s)
+            fwd_row(s)
+
+        at_steps(s, [(1, lambda: join_row(0)), (3, attend)])
+
+        @pl.when(s < 4)
+        def _():
+            fetch_keys(s + 1, 1)
+
+            @pl.when(z + s >= NZ)
+            def _():
+                peer_values(NZ - s)
+                fwd_row(NZ - s)
+
+        at_steps(s, [(2, lambda: join_all(0)), (4, norm_and_grad)])
         return c
 
-    lax.fori_loop(1, NZ, fwd_step, 0)
+    lax.fori_loop(1, 5, fwd_step, 0)
     finish_forward()
 
     def bwd_step(t, c):
@@ -542,10 +516,11 @@
         def _():
             pass_dv(bwd_order(t - 1))
 
+        at_steps(t, [(1, lambda: join_row(1)), (3, lambda: join_all(1)), (5, lin_grads)])
         return c
 
     lax.fori_loop(0, NZ - 1, bwd_step, 0)
-    bwd_diagonal()
+    bwd_row(0, 0)
     spread_dv(0)
 
     @pl.when(up)
@@ -595,24 +570,21 @@
 
         lax.fori_loop(*z_targets(k), gone, 0)
 
-    @pl.when(low)
-    def _():
-        value_to(0, last, last - z, 4).wait_send()
-        row_to(0, last, last - z, 4).wait_send()
+    def passed_on(s, c):
+        def up_gone(*a):
+            value_to(*a).wait_send()
+            row_to(*a, 0).wait_send()
+            row_to(*a, 1).wait_send()
+
+        pl.when(z >= s)(lambda: upward(s, up_gone, True))
+        pl.when((s < 3) & (rem_z(z + s) <= 2))(lambda: downward(s, up_gone, True))
+        return c
+
+    lax.fori_loop(0, 4, passed_on, 0)
 
     def all_gone(d, c):
         @pl.when(z >= d)
         def _():
-            @pl.when((d <= 3) & up)
-            def _():
-                value_to(d, z + 1, d + 1, d).wait_send()
-                row_to(d, z + 1, d + 1, d).wait_send()
-
-            @pl.when(d >= 6)
-            def _():
-                value_to(d, z - 1, d - 1, d).wait_send()
-                row_to(d, z - 1, d - 1, d).wait_send()
-
             for j in range(1, NY):
                 value_to_peer(d, j).wait_send()
                 dv_to_peer(d, j).wait_send()
@@ -625,6 +597,11 @@
         return c
 
     lax.fori_loop(0, NZ, all_gone, 0)
+
+
+def hand_over(*refs):
+    for given, made in zip(refs[:9], refs[9:]):
+        made[...] = given[...]
 
 
 def body(lin_query, lin_key, lin_value, log_decay, norm_gain, lin_gate, lin_grad, soft_query, soft_key, soft_value, soft_grad):
@@ -673,7 +650,7 @@
         vmem((16, TOK), F32),
         vmem((NT, 16, TOK), F32),
         dma((3,)), dma((3,)),
-        dma((NZ,)), dma((NZ,)),
+        dma((2 * NZ,)), dma((2 * NZ,)),
         dma((NZ,)), dma((NZ,)),
         dma((3 * NZ,)), dma((3 * NZ,)),
         dma((6,)), dma((6,)),
@@ -685,9 +662,10 @@
         dma((3 * NZ,)), dma((3 * NZ,)),
         dma((3,)), dma((3,)),
     ]
-    return pl.pallas_call(
+    shapes = [wide] * 7 + [narrow] * 2
+    made = pl.pallas_call(
         kernel,
-        out_shape=[wide] * 7 + [narrow] * 2,
+        out_shape=shapes,
         in_specs=[pl.BlockSpec(memory_space=pltpu.VMEM)] * 11,
         out_specs=[pl.BlockSpec(memory_space=pltpu.VMEM)] * 9,
         scratch_shapes=scratch,
@@ -698,6 +676,13 @@
         lin_query, lin_key, lin_value, log_decay, norm_gain.reshape(1, -1), lin_gate, lin_grad,
         soft_query, soft_key, soft_value, soft_grad,
     )
+    whole = pl.BlockSpec(memory_space=pltpu.VMEM)
+    return pl.pallas_call(
+        hand_over,
+        out_shape=shapes,
+        in_specs=[whole] * 9,
+        out_specs=[whole] * 9,
+    )(*made)
 
 
 def solution(mesh):

time: 126 us -> 110 us (0.87)
  the two profiles are of different devices: /device:TPU:224 before, /device:TPU:2 now
where the time goes in v2:
time: 110 us
  Pallas kernels  109 us (99%)
    pallas_call x1, Pallas kernels, body(): pl.pallas_call(kernel, out_shape=shapes, in_specs=[pl.BlockSpec(memory_sp...  107 us
    pallas_call x1, Pallas kernels, body(): pl.pallas_call(hand_over, out_shape=shapes, in_specs=[whole] * 9, out_spe...  2.73 us

profile of v2, /device:TPU:2, one launch (start us, length us, event | category | flops | bytes accessed | tf_op | source)
XLA Modules:
  0.0 110.0 jit_solution(1663879448191299847)
XLA Ops:
  0.6 106.6 %shard_map.178 = (bf16[256,512]{1,0:T(8,128)(2,1)}, bf16[256,512]{1,0:T(8,128)(2,1)}, bf16[256,512]{1,0:T(8,128)(2,1)}, bf16[256,512]{1,0:T(8,128)(2,1)}, bf16[2...) custom-call(bf16[256,512]{1,0:T(8,128)(2,1)} %lq.1, ...), custom_call_target="tpu_custom_call" | custom-call | tf_op jit(solution)/shard_map/pallas_call | solution.py:666
  107.3 2.7 %shard_map.179 = (bf16[256,512]{1,0:T(8,128)(2,1)}, bf16[256,512]{1,0:T(8,128)(2,1)}, bf16[256,512]{1,0:T(8,128)(2,1)}, bf16[256,512]{1,0:T(8,128)(2,1)}, bf16[2...) custom-call(bf16[256,512]{1,0:T(8,128)(2,1)} %get-tuple-element.18.r, ...), custom_call_target="tpu_custom_call" | custom-call | tf_op jit(solution)/shard_map/pallas_call | solution.py:680

commit v3 on v2

--- a/solution.py
+++ b/solution.py
@@ -47,7 +47,7 @@
     lin_out, dlq, dlk, dlv, dgate, sout, dsq, dsk, dsv,
     kall, vall, q_t, g_t, v_t, k_t, peak, total, out_t, log_s, delta_s, dq_t, dk_acc, dv_acc,
     dks, dkr, dvs, dvy, dv_own, dvz, dvr, dky,
-    decay, weights, gweights, tail_s, lead_s, att, gr_att, msg, st, pre, lead_tot, rmsg, rst, cmsg, car, tps, tpr,
+    decay, weights, gweights, tail_s, lead_s, att, gr_att, msg, st, pre, lead_tot, row_state, row_tot, before, before_tot, bsum, binc, cmsg, car, tps, tpr,
     ky_s, ky_r, ks_s, kr_r, vs_s, vr_r, vy_s, vy_r, p1_s, p1_r, p2_s, p2_r, p3_s, p3_r, tp_s, tp_r,
     dk_s, dk_r, dv_s, dv_r, dvy_s, dvy_r, dky_s, dky_r,
 ):
@@ -144,17 +144,17 @@
                     value_to_peer(NZ - s, j).start()
 
     def fetch_keys(s, half):
-        @pl.when(z >= s)
+        @pl.when((s <= 4 - half) & (z >= s))
         def _():
             at = s * 2 + half
             arrived(kall.at[half_of(z - s, half)], kr_r.at[at], ks_s.at[at])
-            upward(s, lambda *a: row_to(*a, half).start(), s < 4)
-
-        @pl.when((s <= 3) & (rem_z(z + s) <= 2))
+            upward(s, lambda *a: row_to(*a, half).start(), s < 4 - half)
+
+        @pl.when((s <= 3 + half) & (rem_z(z + s) <= 2 + half))
         def _():
             at = (s + 4) * 2 + half
             arrived(kall.at[half_of(rem_z(z + s), half)], kr_r.at[at], ks_s.at[at])
-            downward(s, lambda *a: row_to(*a, half).start(), s < 3)
+            downward(s, lambda *a: row_to(*a, half).start(), s < 3 + half)
 
     def peer_values(d):
         for j in range(1, NY):
@@ -180,7 +180,7 @@
 
     for half in range(2):
         upward(0, lambda *a: row_to(*a, half).start(), True)
-        downward(0, lambda *a: row_to(*a, half).start(), low)
+        downward(0, lambda *a: row_to(*a, half).start(), z <= 2 + half)
 
     def coded(tot):
         first = tot.astype(BF16).astype(F32)
@@ -197,8 +197,37 @@
         at = k * 3 + j - 1
         return copy(msg.at[k, y_peer(j)], st.at[k, y], p1_s.at[at], p1_r.at[at], at_ctx(z, y_peer(j)))
 
-    def total_to(k, zz):
-        return copy(rmsg.at[k], rst.at[k, z], p2_s.at[k * NZ + zz], p2_r.at[k * NZ + z], at_ctx(zz, y))
+    def order(k):
+        return z if k == 0 else NZ - 1 - z
+
+    def block_sum_to(k, step, j):
+        to = lax.rem(order(k) + 1 + j, NZ)
+        to_z = to if k == 0 else NZ - 1 - to
+        at = k * 3 + step
+        return copy(bsum.at[at], binc.at[at], p2_s.at[at * 4 + j], p2_r.at[at], at_ctx(to_z, y))
+
+    def gives(k, step):
+        return lax.rem(order(k), 2 << step) == (1 << step) - 1
+
+    def takes(k, step):
+        return lax.rem(lax.div(order(k), 1 << step), 2) == 1
+
+    def give(k, step):
+        @pl.when(gives(k, step))
+        def _():
+            at = k * 3 + step
+            bsum[at, :DH, :] = (jnp.exp(row_tot[...]) * before[...] + row_state[...]).astype(BF16)
+            bsum[at, DH:, :] = coded(before_tot[...] + row_tot[...])
+            for j in range(1 << step):
+                block_sum_to(k, step, j).start()
+
+    def take(k, step):
+        @pl.when(takes(k, step))
+        def _():
+            at = k * 3 + step
+            arrived(binc.at[at], p2_r.at[at], p2_s.at[at * 4])
+            before[...] = jnp.exp(before_tot[...]) * binc[at, :DH, :].astype(F32) + before[...]
+            before_tot[...] = before_tot[...] + decoded(binc[at, DH:, :])
 
     def carried_to_peer(k, j):
         at = k * 3 + j - 1
@@ -208,9 +237,6 @@
         st[k, y] = msg[k, y]
         for j in range(1, NY):
             state_to_peer(k, j).start()
-
-    def z_targets(k):
-        return (z + 1, NZ) if k == 0 else (0, z)
 
     def join_row(k):
         for j in range(1, NY):
@@ -225,25 +251,20 @@
             tot = decoded(st[k, i, DH:, :])
             state = jnp.exp(tot) * state + st[k, i, :DH, :].astype(F32)
             so_far = so_far + tot
-        rmsg[k, :DH, :] = state.astype(BF16)
-        rmsg[k, DH:, :] = coded(so_far)
-
-        def one(zz, c):
-            total_to(k, zz).start()
-            return c
-
-        lax.fori_loop(*z_targets(k), one, 0)
+        row_state[...] = state
+        row_tot[...] = so_far
+        before[...] = jnp.zeros((DH, DH), F32)
+        before_tot[...] = jnp.zeros((1, DH), F32)
+        give(k, 0)
+
+    def join_blocks(k, step):
+        take(k, step)
+        give(k, step + 1)
 
     def join_all(k):
-        def one(i, state):
-            zz = i if k == 0 else NZ - 1 - i
-            at = k * NZ + zz
-            arrived(rst.at[k, zz], p2_r.at[at], p2_s.at[at])
-            return jnp.exp(decoded(rst[k, zz, DH:, :])) * state + rst[k, zz, :DH, :].astype(F32)
-
-        state = lax.fori_loop(0, z if k == 0 else NZ - 1 - z, one, jnp.zeros((DH, DH), F32))
+        take(k, 2)
         for i in range(NY):
-            cmsg[k, i] = (pre[i] + jnp.exp(lead_tot[i]) * state).astype(BF16)
+            cmsg[k, i] = (pre[i] + jnp.exp(lead_tot[i]) * before[...]).astype(BF16)
         car[k, y] = cmsg[k, y]
         for j in range(1, NY):
             carried_to_peer(k, j).start()
@@ -396,18 +417,28 @@
     def local_block(yy):
         return pl.ds(pl.multiple_of(yy * TOK, TOK), TOK)
 
-    def target(d):
-        near = d <= 4
+    def target(d, half=0):
+        near = d <= 4 - half
         to_z = jnp.where(near, z - 1, jnp.where(up, z + 1, z - d))
         slot = jnp.where(near, d - 1, jnp.where(up, d + 1, 4))
         return to_z, slot
 
-    def has_incoming(d):
-        return ((d <= 3) & up) | (d >= 6)
-
-    def dk_copy(d):
-        to_z, slot = target(d)
-        return copy(dks.at[d], dkr.at[slot], dk_s.at[d], dk_r.at[slot], at_ctx(to_z, y))
+    def has_incoming(d, half=0):
+        return ((d <= 3 - half) & up) | (d >= 6 - half)
+
+    def half_row(half):
+        return pl.ds(half * (ROW // 2), ROW // 2)
+
+    def dk_copy(d, half):
+        to_z, slot = target(d, half)
+        src, dst = dks.at[d, half_row(half)], dkr.at[slot, half_row(half)]
+        return copy(src, dst, dk_s.at[d * 2 + half], dk_r.at[slot * 2 + half], at_ctx(to_z, y))
+
+    def add_dk(slot, half):
+        at = slot * 2 + half
+        rows = half_row(half)
+        arrived(dkr.at[slot, rows], dk_r.at[at], dk_s.at[at])
+        dk_acc[rows, :] = dk_acc[rows, :] + dkr[slot, rows, :].astype(F32)
 
     def dv_copy(d):
         to_z, slot = target(d)
@@ -441,12 +472,11 @@
         acc[...] = acc[...] + slots[slot].astype(F32)
 
     def pass_dk(d):
-        @pl.when(has_incoming(d))
-        def _():
-            add_incoming(dk_acc, dkr, dk_r, dk_s, d)
-
-        dks[d] = dk_acc[...].astype(BF16)
-        dk_copy(d).start()
+        for half in range(2):
+            pl.when(has_incoming(d, half))(lambda: add_dk(d, half))
+            rows = half_row(half)
+            dks[d, rows, :] = dk_acc[rows, :].astype(BF16)
+            dk_copy(d, half).start()
 
     part = dv_acc.at[pl.ds(0, TOK)]
 
@@ -486,7 +516,7 @@
             peer_values(s)
             fwd_row(s)
 
-        at_steps(s, [(1, lambda: join_row(0)), (3, attend)])
+        at_steps(s, [(1, lambda: join_row(0))])
 
         @pl.when(s < 4)
         def _():
@@ -497,7 +527,7 @@
                 peer_values(NZ - s)
                 fwd_row(NZ - s)
 
-        at_steps(s, [(2, lambda: join_all(0)), (4, norm_and_grad)])
+        at_steps(s, [(1, lambda: join_blocks(0, 0)), (2, lambda: join_blocks(0, 1)), (3, lambda: join_all(0)), (4, lambda: attend())])
         return c
 
     lax.fori_loop(1, 5, fwd_step, 0)
@@ -516,7 +546,7 @@
         def _():
             pass_dv(bwd_order(t - 1))
 
-        at_steps(t, [(1, lambda: join_row(1)), (3, lambda: join_all(1)), (5, lin_grads)])
+        at_steps(t, [(0, lambda: norm_and_grad()), (1, lambda: join_row(1)), (2, lambda: join_blocks(1, 0)), (3, lambda: join_blocks(1, 1)), (4, lambda: join_all(1)), (6, lambda: lin_grads())])
         return c
 
     lax.fori_loop(0, NZ - 1, bwd_step, 0)
@@ -525,11 +555,11 @@
 
     @pl.when(up)
     def _():
-        add_incoming(dk_acc, dkr, dk_r, dk_s, 0)
-
-    @pl.when(low)
-    def _():
-        add_incoming(dk_acc, dkr, dk_r, dk_s, 4)
+        add_dk(0, 0)
+        add_dk(0, 1)
+
+    for half in range(2):
+        pl.when(z <= 2 + half)(lambda: add_dk(4, half))
 
     dks[0] = dk_acc[...].astype(BF16)
     for j in range(1, NY):
@@ -563,21 +593,20 @@
     for j in range(1, NT):
         sums_to(j).wait_send()
     for k in range(2):
-
-        def gone(zz, c, k=k):
-            total_to(k, zz).wait_send()
-            return c
-
-        lax.fori_loop(*z_targets(k), gone, 0)
+        for step in range(3):
+
+            @pl.when(gives(k, step))
+            def _():
+                for j in range(1 << step):
+                    block_sum_to(k, step, j).wait_send()
 
     def passed_on(s, c):
-        def up_gone(*a):
-            value_to(*a).wait_send()
-            row_to(*a, 0).wait_send()
-            row_to(*a, 1).wait_send()
-
-        pl.when(z >= s)(lambda: upward(s, up_gone, True))
-        pl.when((s < 3) & (rem_z(z + s) <= 2))(lambda: downward(s, up_gone, True))
+        pl.when(z >= s)(lambda: upward(s, lambda *a: value_to(*a).wait_send(), True))
+        pl.when((s < 3) & (rem_z(z + s) <= 2))(lambda: downward(s, lambda *a: value_to(*a).wait_send(), True))
+        for half in range(2):
+            gone = lambda *a: row_to(*a, half).wait_send()
+            pl.when(z >= s)(lambda: upward(s, gone, s < 4 - half))
+            pl.when(rem_z(z + s) <= 2 + half)(lambda: downward(s, gone, s < 3 + half))
         return c
 
     lax.fori_loop(0, 4, passed_on, 0)
@@ -591,7 +620,8 @@
 
             @pl.when(d >= 1)
             def _():
-                dk_copy(d).wait_send()
+                dk_copy(d, 0).wait_send()
+                dk_copy(d, 1).wait_send()
                 dv_copy(d).wait_send()
 
         return c
@@ -643,21 +673,25 @@
         vmem((2, NY, MSG, DH), BF16),
         vmem((NY, DH, DH), F32),
         vmem((NY, 1, DH), F32),
-        vmem((2, MSG, DH), BF16),
-        vmem((2, NZ, MSG, DH), BF16),
+        vmem((DH, DH), F32),
+        vmem((1, DH), F32),
+        vmem((DH, DH), F32),
+        vmem((1, DH), F32),
+        vmem((6, MSG, DH), BF16),
+        vmem((6, MSG, DH), BF16),
         vmem((2, NY, DH, DH), BF16),
         vmem((2, HEADS, DH, DH), BF16),
         vmem((16, TOK), F32),
         vmem((NT, 16, TOK), F32),
         dma((3,)), dma((3,)),
-        dma((2 * NZ,)), dma((2 * NZ,)),
+        dma((2 * NZ + 2,)), dma((2 * NZ + 2,)),
         dma((NZ,)), dma((NZ,)),
         dma((3 * NZ,)), dma((3 * NZ,)),
         dma((6,)), dma((6,)),
-        dma((2 * NZ,)), dma((2 * NZ,)),
+        dma((24,)), dma((6,)),
         dma((6,)), dma((6,)),
         dma((NT - 1,)), dma((NT - 1,)),
-        dma((NZ,)), dma((NZ,)),
+        dma((2 * NZ,)), dma((2 * NZ,)),
         dma((NZ,)), dma((NZ,)),
         dma((3 * NZ,)), dma((3 * NZ,)),
         dma((3,)), dma((3,)),

time: 110 us -> 104 us (0.945)
  Pallas kernels: 109 us -> 102 us
    pallas_call x1, Pallas kernels: 107 us -> 99.6 us  [body(): pl.pallas_call(kernel, out_shape=shapes, in_specs=[pl.BlockSpec(memory_sp...]
where the time goes in v3:
time: 104 us; the launch traced here: 103 us
  Pallas kernels  102 us (98%)
    pallas_call x1, Pallas kernels, body(): pl.pallas_call(kernel, out_shape=shapes, in_specs=[pl.BlockSpec(memory_sp...  99.6 us
    pallas_call x1, Pallas kernels, body(): pl.pallas_call(hand_over, out_shape=shapes, in_specs=[whole] * 9, out_spe...  2.73 us

profile of v3, /device:TPU:2, one launch (start us, length us, event | category | flops | bytes accessed | tf_op | source)
XLA Modules:
  0.0 103.0 jit_solution(665432858612419230)
XLA Ops:
  0.6 99.6 %shard_map.178 = (bf16[256,512]{1,0:T(8,128)(2,1)}, bf16[256,512]{1,0:T(8,128)(2,1)}, bf16[256,512]{1,0:T(8,128)(2,1)}, bf16[256,512]{1,0:T(8,128)(2,1)}, bf16[2...) custom-call(bf16[256,512]{1,0:T(8,128)(2,1)} %lq.1, ...), custom_call_target="tpu_custom_call" | custom-call | tf_op jit(solution)/shard_map/pallas_call | solution.py:700
  100.3 2.7 %shard_map.179 = (bf16[256,512]{1,0:T(8,128)(2,1)}, bf16[256,512]{1,0:T(8,128)(2,1)}, bf16[256,512]{1,0:T(8,128)(2,1)}, bf16[256,512]{1,0:T(8,128)(2,1)}, bf16[2...) custom-call(bf16[256,512]{1,0:T(8,128)(2,1)} %get-tuple-element.18.r, ...), custom_call_target="tpu_custom_call" | custom-call | tf_op jit(solution)/shard_map/pallas_call | solution.py:714

commit v4 on v3

--- a/solution.py
+++ b/solution.py
@@ -506,11 +506,16 @@
             pl.when(now == at)(event)
 
     def fwd_step(s, c):
-        @pl.when(s < 4)
+        @pl.when(s < 3)
         def _():
             fetch_values(s + 1)
             fetch_keys(s + 1, 0)
 
+        @pl.when(s == 4)
+        def _():
+            fetch_keys(4, 0)
+            fetch_keys(4, 1)
+
         @pl.when(z >= s)
         def _():
             peer_values(s)
@@ -518,9 +523,11 @@
 
         at_steps(s, [(1, lambda: join_row(0))])
 
+        pl.when(s < 3)(lambda: fetch_keys(s + 1, 1))
+        pl.when(s == 3)(lambda: fetch_values(4))
+
         @pl.when(s < 4)
         def _():
-            fetch_keys(s + 1, 1)
 
             @pl.when(z + s >= NZ)
             def _():

time: 104 us -> 104 us (level)
  no operation moved by 1% of the time
where the time goes in v4:
time: 104 us; the launch traced here: 102 us
  Pallas kernels  102 us (98%)
    pallas_call x1, Pallas kernels, body(): pl.pallas_call(kernel, out_shape=shapes, in_specs=[pl.BlockSpec(memory_sp...  99 us
    pallas_call x1, Pallas kernels, body(): pl.pallas_call(hand_over, out_shape=shapes, in_specs=[whole] * 9, out_spe...  2.73 us

profile of v4, /device:TPU:2, one launch (start us, length us, event | category | flops | bytes accessed | tf_op | source)
XLA Modules:
  0.0 102.4 jit_solution(14404477692810143187)
XLA Ops:
  0.6 99.0 %shard_map.178 = (bf16[256,512]{1,0:T(8,128)(2,1)}, bf16[256,512]{1,0:T(8,128)(2,1)}, bf16[256,512]{1,0:T(8,128)(2,1)}, bf16[256,512]{1,0:T(8,128)(2,1)}, bf16[2...) custom-call(bf16[256,512]{1,0:T(8,128)(2,1)} %lq.1, ...), custom_call_target="tpu_custom_call" | custom-call | tf_op jit(solution)/shard_map/pallas_call | solution.py:707
  99.7 2.7 %shard_map.179 = (bf16[256,512]{1,0:T(8,128)(2,1)}, bf16[256,512]{1,0:T(8,128)(2,1)}, bf16[256,512]{1,0:T(8,128)(2,1)}, bf16[256,512]{1,0:T(8,128)(2,1)}, bf16[2...) custom-call(bf16[256,512]{1,0:T(8,128)(2,1)} %get-tuple-element.18.r, ...), custom_call_target="tpu_custom_call" | custom-call | tf_op jit(solution)/shard_map/pallas_call | solution.py:721
